TPU v7x, 128 devices: a whole 4x4x4 slice. The times are simulated.
128 devices in a mesh: row: 16 (over y_lo, x, core), col: 8 (over z, y_hi).
Axes of the slice: x: 4, y: 4 (y_hi: 2, y_lo: 2; y = y_hi * 2 + y_lo), z: 4, core: 2. Of those that a mesh axis runs over, the one named last changes fastest.
Arguments:
- x_blocks: float32 [256, 32, 4096], P('row', 'col'), may hold values from -1 to 1, as said below
- block_cols: int32 [256, 32], P('row', 'col'), may hold values from -1 to 255, as said below
Outputs:
- square: float32 [256, 32, 4096], P('row', 'col')
- updated: float32 [256, 32, 4096], P('row', 'col')
Inputs may be any that keep to these rules, and one draw needn't show every extreme that they name: `block_cols`: slots (c * 4) to (c * 4 + 3) of a block row hold distinct block columns of group c, that is columns c * 256 // 8 to (c + 1) * 256 // 8 - 1, in increasing order, with the empty slots (-1) last. Every block row holds its own column, holds at most 15 columns, and the pattern is symmetric: row i holds column j exactly when row j holds column i. `x_blocks`: the matrix is symmetric: the block of row j at the slot of column i is the transpose of the block of row i at the slot of column j. Its spectral norm is below one. Empty slots hold zeros.
All inputs are finite; a program needn't handle non-finite values.
Results may differ from a plain program's by a relative error of at most 0.0003.
Values sent between devices are 32-bit elements; how exact they have to be, the bound alone decides.
A program may use at most 128 MiB of HBM per device.

v0:
```python
import jax
import jax.numpy as jnp
from jax import lax
from jax.sharding import PartitionSpec as P

BS = 64
BAND = 7


def pack_slots(left_vals, left_cols, usable, limit):
    slot_count = left_cols.shape[0]
    slot_index = jnp.arange(slot_count, dtype=jnp.int32)
    order = jnp.cumsum(usable.astype(jnp.int32)) - 1
    places = jnp.arange(limit, dtype=jnp.int32)
    picked = usable[None, :] & (order[None, :] == places[:, None])
    found = jnp.any(picked, axis=1)
    index = jnp.sum(jnp.where(picked, slot_index[None, :], 0), axis=1)
    packed_vals = jnp.where(found[:, None], left_vals[index], 0.0)
    packed_cols = jnp.where(found, left_cols[index], -1)
    return (packed_vals, packed_cols, found)


def pick_blocks(panel_vals, panel_cols, right_rows, own_row, left_found):
    right_cols = panel_cols[right_rows]
    slot_count = right_cols.shape[1]
    slot_index = jnp.arange(slot_count, dtype=jnp.int32)
    lined = (
        (right_cols[:, None, :] == own_row[None, :, None])
        & (own_row >= 0)[None, :, None]
        & left_found[:, None, None]
    )
    where_u = jnp.sum(jnp.where(lined, slot_index[None, None, :], 0), axis=2)
    present = jnp.any(lined, axis=2)
    chosen = panel_vals[right_rows[:, None], where_u]
    return jnp.where(present[:, :, None], chosen, 0.0)


def multiply_rows(left_vals, chosen):
    leading = left_vals.shape[0]
    own_slots = chosen.shape[1]
    result = jnp.einsum(
        "tab,tsbc->sac",
        left_vals.reshape(leading, BS, BS),
        chosen.reshape(leading, own_slots, BS, BS),
        precision=lax.Precision.HIGHEST,
    )
    return result.reshape(own_slots, BS * BS)


def panel_product(row_vals, row_cols, own_cols, panel_vals, panel_cols):
    limit = min(2 * BAND + 1, row_cols.shape[1])

    def one_row(packed):
        left_vals, left_cols, own_row = packed
        kept_vals, kept_cols, found = pack_slots(left_vals, left_cols, left_cols >= 0, limit)
        right_rows = jnp.where(found, kept_cols, 0).astype(jnp.int32)
        chosen = pick_blocks(panel_vals, panel_cols, right_rows, own_row, found)
        return multiply_rows(kept_vals, chosen)

    return lax.map(one_row, (row_vals, row_cols, own_cols))


def local(x_blocks, block_cols):
    cleaned = jnp.where((block_cols >= 0)[:, :, None], x_blocks, jnp.zeros_like(x_blocks))
    row_vals, row_cols = (
        lax.all_gather(cleaned, "col", axis=1, tiled=True),
        lax.all_gather(block_cols, "col", axis=1, tiled=True),
    )
    panel_vals, panel_cols = (
        lax.all_gather(cleaned, "row", axis=0, tiled=True),
        lax.all_gather(block_cols, "row", axis=0, tiled=True),
    )
    square = panel_product(row_vals, row_cols, block_cols, panel_vals, panel_cols)
    square_vals = lax.all_gather(square, "row", axis=0, tiled=True)
    second = panel_product(row_vals, row_cols, block_cols, square_vals, panel_cols)
    updated = 1.5 * cleaned - 0.5 * second
    return (square, updated)


def solution(mesh):
    return jax.shard_map(
        local,
        mesh=mesh,
        in_specs=(P("row", "col", None), P("row", "col")),
        out_specs=(P("row", "col", None), P("row", "col", None)),
        check_vma=False,
    )
```

profile of v0, /device:TPU:1, one launch (start us, length us, event | category | flops | bytes accessed | tf_op | source)
XLA Modules:
  0.0 763.5 jit_solution(13560598982049736104)
XLA Ops:
  12.1 21.3 %all-gather.1 = s32[16,16,4]{1,2,0:T(4,128)S(1)} all-gather(s32[1,16,4]{1,2,0:T(4,128)S(1)} %bitcast.137), channel_id=1, replica_groups=mesh['row'=16,'col'=8] {'row'}, dimensions={0}, use_global_device_ids=true | all-gather | bytes 4352 | tf_op jit(solution)/shard_map/all_gather | solution.py:71
  33.5 26.9 %all-gather = s32[8,4,16]{2,1,0:T(4,128)S(1)} all-gather(s32[1,4,16]{2,1,0:T(4,128)S(1)} %bitcast.138), channel_id=1, replica_groups=mesh['row'=16,'col'=8] {'col'}, dimensions={0}, use_global_device_ids=true | all-gather | bytes 2304 | tf_op jit(solution)/shard_map/all_gather | solution.py:67
  60.4 61.0 %all-gather.8.cloned.1.call-done = f32[16,32,4096]{2,0,1:T(8,128)} async-done(((f32[16,4,4096]{2,0,1:T(8,128)}), f32[16,32,4096]{2,0,1:T(8,128)}) %all-gather.8.cloned.1.call-update) | async-done | bytes 8388624 | tf_op jit(solution)/shard_map/all_gather | solution.py:66
  121.5 11.7 %copy.63 = f32[16,32,4096]{2,1,0:T(8,128)} copy(f32[16,32,4096]{2,0,1:T(8,128)} %all-gather.8.cloned.1.call-done) | data formatting | bytes 16777216 | tf_op jit(solution)/shard_map/while | solution.py:60
  133.2 80.7 %all-gather.6.cloned.1.call-done = f32[256,4,4096]{2,1,0:T(4,128)} async-done(((f32[16,4,4096]{2,1,0:T(4,128)}), f32[256,4,4096]{2,1,0:T(4,128)}) %all-gather.6.cloned.1.call-update) | async-done | bytes 16777232 | tf_op jit(solution)/shard_map/all_gather | solution.py:70
  215.1 221.1 %while.24 = (s32[]{:T(128)}, f32[16,4,4096]{2,1,0:T(4,128)}, s32[16,32]{1,0:T(8,128)S(1)}, s32[256,4]{1,0:T(8,128)S(1)}, s32[16,4]{1,0:T(8,128)S(1)}, /*index=5*...) while((s32[]{:T(128)}, f32[16,4,4096]{2,1,0:T(4,128)}, s32[16,32]{1,0:T(8,128)S(1)}, ...), condition=%wide.region_6.7_spmd, body=%wide.region_0.6_spmd.sunk | while | flops 189059264 | bytes 9632848 | solution.py:60
  217.3 2.7 gather_fusion.2
  220.0 2.1 gather.90
  230.9 2.8 gather_fusion.2
  244.6 2.6 gather_fusion.2
  247.2 2.1 gather.90
  258.1 3.0 gather_fusion.2
  261.0 2.1 gather.90
  271.9 2.7 gather_fusion.2
  285.5 3.2 gather_fusion.2
  299.6 2.8 gather_fusion.2
  313.3 3.1 gather_fusion.2
  327.3 2.9 gather_fusion.2
  330.2 2.1 gather.90
  341.1 3.3 gather_fusion.2
  344.4 2.1 gather.90
  355.2 2.7 gather_fusion.2
  358.0 2.1 gather.90
  368.9 3.5 gather_fusion.2
  372.4 2.1 gather.90
  383.2 2.9 gather_fusion.2
  397.0 3.1 gather_fusion.2
  410.9 3.0 gather_fusion.2
  424.8 2.7 gather_fusion.2
  436.2 95.5 %all-gather.10.cloned.1.call-done = f32[256,4,4096]{2,1,0:T(4,128)} async-done(((f32[16,4,4096]{2,1,0:T(4,128)}), f32[256,4,4096]{2,1,0:T(4,128)}) %all-gather.10.cloned.1.call-update) | async-done | bytes 16777232 | tf_op jit(solution)/shard_map/all_gather | solution.py:74
  532.9 221.1 %while.25 = (s32[]{:T(128)}, f32[16,4,4096]{2,1,0:T(4,128)}, s32[16,32]{1,0:T(8,128)S(1)}, s32[256,4]{1,0:T(8,128)S(1)}, s32[16,4]{1,0:T(8,128)S(1)}, /*index=5*...) while((s32[]{:T(128)}, f32[16,4,4096]{2,1,0:T(4,128)}, s32[16,32]{1,0:T(8,128)S(1)}, ...), condition=%wide.region_13.14_spmd, body=%wide.region_7.13_spmd.sunk | while | flops 189059264 | bytes 9632848 | solution.py:60
  535.1 2.7 gather_fusion.6
  548.6 2.8 gather_fusion.6
  562.3 2.6 gather_fusion.6
  575.9 3.0 gather_fusion.6
  589.7 2.7 gather_fusion.6
  603.3 3.2 gather_fusion.6
  617.4 2.8 gather_fusion.6
  631.1 3.1 gather_fusion.6
  645.1 2.9 gather_fusion.6
  658.9 3.3 gather_fusion.6
  673.0 2.7 gather_fusion.6
  686.6 3.5 gather_fusion.6
  701.0 2.9 gather_fusion.6
  714.8 3.1 gather_fusion.6
  728.7 3.0 gather_fusion.6
  742.6 2.7 gather_fusion.6
  754.0 3.0 multiply_subtract_fusion
  (972 shorter events, 337.1 us)
Async XLA Ops:
  7.2 114.3 %all-gather.8.cloned.1.call-start = ((), (), s32[]{:S(2)}) async-start(), calls=%async_computation.1 | async-start | bytes 9437184 | tf_op jit(solution)/shard_map/all_gather | solution.py:66
  9.5 1.7 copy-start
  9.6 2.4 copy-start.1
  11.2 202.7 %all-gather.6.cloned.1.call-start = ((), (), s32[]{:S(2)}) async-start(), calls=%async_computation | async-start | bytes 17825792 | tf_op jit(solution)/shard_map/all_gather | solution.py:70
  11.9 519.8 %all-gather.10.cloned.1.call-start = ((), (), s32[]{:S(2)}) async-start(), calls=%async_computation.2 | async-start | bytes 17825792 | tf_op jit(solution)/shard_map/all_gather | solution.py:74
Sparse Core Ops, SparseCore 0:
  11.3 110.1 all-gather.7
  123.8 90.1 all-gather.5
  436.3 95.2 all-gather.9
where the time goes:
time: 772 us; the launch traced here: 764 us
  local copies, waits for them, and re-layouts  377 us (49%)
  waiting for transfers between devices  238 us (31%)
  matrix products  58.9 us (8%)
  blocking collectives  48.1 us (6%)
  other arithmetic  23.9 us (3%)
  between operations  13.8 us (2%)
    gather x96, local copies, waits for them, and re-layouts, pick_blocks(): chosen = panel_vals[right_rows[:, None], where_u]  222 us
    all_gather x1, waiting for transfers between devices, local(): square_vals = lax.all_gather(square, 'row', axis=0, tiled=True)  95.5 us
    all_gather x1, waiting for transfers between devices, local(): lax.all_gather(cleaned, 'row', axis=0, tiled=True)  80.7 us
    all_gather x1, waiting for transfers between devices, local(): lax.all_gather(cleaned, 'col', axis=1, tiled=True)  61 us
    dot_general x32, matrix products, multiply_rows(): jnp.einsum('tab,tsbc->sac', left_vals.reshape(leading, BS, BS), chosen.re...  58.9 us
    squeeze x64, local copies, waits for them, and re-layouts, panel_product(): return lax.map(one_row, (row_vals, row_cols, own_cols))  35 us
    all_gather x1, blocking collectives, local(): lax.all_gather(block_cols, 'col', axis=1, tiled=True)  26.9 us
    gather x64, local copies, waits for them, and re-layouts, pack_slots(): packed_vals = jnp.where(found[:, None], left_vals[index], 0.0)  26.5 us
  transfers between devices with their start and end apart: 3, of which 3 were waited for; matrix products, arithmetic and copies ran while one was open for 2% of the time, Pallas kernels for 0%

commit v1 on v0

v1 whole, which is shorter than its diff:
```python
import heapq

import jax
import jax.numpy as jnp
from jax import lax
from jax.experimental import pallas as pl
from jax.experimental.pallas import tpu as pltpu
from jax.sharding import PartitionSpec as P

MESH = pl.DeviceIdType.MESH

ROWS = 16
KC = 4
N_R = 16
N_C = 8
PIECES = 8
STEP = ROWS // PIECES
PIECE_US = 23.0 / PIECES
HOP_US = 1.5
COLS = PIECES

OWN = (0, 0)
MESSAGES = [(d, p) for d in range(4) for p in range(2)]


def slot(message):
    return message[0] * 2 + message[1]


def tree(piece, pair_first):
    def route(message):
        d, p = message
        if d == 2:
            forward = (piece + (p if pair_first else 0)) % 2 == 0
            ring = ["+", "+"] if forward else ["-", "-"]
        else:
            ring = [[], ["+"], None, ["-"]][d]
        pair = ["pair"] * p
        return tuple(pair + ring if pair_first else ring + pair)

    by_route = {route(m): m for m in MESSAGES}
    children = {m: [] for m in MESSAGES}
    for m in MESSAGES:
        if m != OWN:
            r = route(m)
            children[by_route[r[:-1]]].append((r[-1], m))
    return children


def plan(gathers):
    free = {}
    order = []
    queue = []
    count = 0
    for name, trees, links in gathers:
        for piece in [COLS] + list(range(PIECES)):
            count += 1
            heapq.heappush(queue, (0.01 * (piece + 1) if piece != COLS else 0.0, count, name, OWN, piece))
    table = {name: (trees, links) for name, trees, links in gathers}
    while queue:
        now, _, name, message, piece = heapq.heappop(queue)
        if message != OWN:
            order.append((now, name, message, piece))
        trees, links = table[name]
        for link, child in trees[piece][message]:
            wire = links[link]
            start = max(now, free.get(wire, 0.0))
            free[wire] = start + (0.05 if piece == COLS else PIECE_US)
            count += 1
            heapq.heappush(queue, (free[wire] + HOP_US, count, name, child, piece))
    return sorted(order, key=lambda e: e[0])


def trees_of(pair_first):
    return [tree(k, pair_first[k]) for k in range(PIECES)] + [tree(0, True)]


R_TREES = trees_of([k % 4 != 3 for k in range(PIECES)])
L_TREES = trees_of([True] * PIECES)
S_TREES = trees_of([k % 8 not in (2, 5, 7) for k in range(PIECES)])
R_LINKS = {"+": "x+", "-": "x-", "pair": "y"}
L_LINKS = {"+": "z+", "-": "z-", "pair": "y"}


class Place:
    def __init__(self):
        self.r = lax.axis_index("row")
        self.c = lax.axis_index("col")
        self.core = self.r % 2
        self.x = (self.r // 2) % 4
        self.yl = self.r // 8
        self.z = self.c // 2
        self.yh = self.c % 2
        self.q = self.r // 2

    def row_of(self, x, yl, core):
        return (yl * 4 + x) * 2 + core

    def row_source(self, message):
        d, p = message
        yl = 1 - self.yl if p else self.yl
        return self.row_of((self.x + 4 - d) % 4, yl, self.core)

    def col_source(self, message):
        d, p = message
        yh = 1 - self.yh if p else self.yh
        return ((self.z + 4 - d) % 4) * 2 + yh

    def row_neighbour(self, link):
        if link == "pair":
            return (self.row_of(self.x, 1 - self.yl, self.core), self.c)
        return (self.row_of((self.x + (1 if link == "+" else 3)) % 4, self.yl, self.core), self.c)

    def col_neighbour(self, link):
        if link == "pair":
            return (self.r, self.z * 2 + 1 - self.yh)
        return (self.r, ((self.z + (1 if link == "+" else 3)) % 4) * 2 + self.yh)

    def sibling(self):
        return (self.row_of(self.x, self.yl, 1 - self.core), self.c)


def remote(ref, send, recv, device, to=None):
    return pltpu.make_async_remote_copy(
        src_ref=ref,
        dst_ref=ref if to is None else to,
        send_sem=send,
        recv_sem=recv,
        device_id=device,
        device_id_type=MESH,
    )


def kernel(
    x_ref, tile_ref, cs_ref, sq_ref, up_ref,
    rp, lp, acc, pc, lc, pc_s, lc_s,
    send, cols_send, r_recv, l_recv, s_recv, r_sib, s_sib, pair_sem, local_sem,
    *sp,
):
    place = Place()
    r, c, q = place.r, place.c, place.q
    sibling = place.sibling()
    lane = lax.broadcasted_iota(jnp.int32, (64, 128), 1)
    lane_half = lax.broadcasted_iota(jnp.int32, (32, 128), 1) < 64

    barrier = pltpu.get_barrier_semaphore()
    neighbours = [place.row_neighbour(k) for k in ("+", "-", "pair")]
    neighbours += [place.col_neighbour(k) for k in ("+", "-", "pair")] + [sibling]
    for device in neighbours:
        pl.semaphore_signal(barrier, inc=1, device_id=device, device_id_type=MESH)

    def convert(i, carry):
        for h in range(2):
            pair = []
            for u in (2 * h, 2 * h + 1):
                v = x_ref[i, pl.ds(u, 32, stride=4), :]
                pair.append(jnp.where(cs_ref[i * KC + u] >= 0, v, 0.0))
            even = jnp.where(lane_half, pair[0], pltpu.roll(pair[1], 64, 1))
            odd = jnp.where(lane_half, pltpu.roll(pair[0], 64, 1), pair[1])
            for panel, n in ((rp, r), (lp, c)):
                panel[n, i, h, pl.ds(0, 32, stride=2), :] = even
                panel[n, i, h, pl.ds(1, 32, stride=2), :] = odd
        return carry

    lax.fori_loop(0, ROWS, convert, 0)
    pc[q, place.core] = tile_ref[...]
    lc[c] = tile_ref[...]
    pl.semaphore_wait(barrier, len(neighbours))

    def ref_of(name, message, piece):
        if name == "L":
            n = place.col_source(message)
            return lc.at[n] if piece == COLS else lp.at[n, pl.ds(piece * STEP, STEP)]
        if name == "S":
            return sp[slot(message)].at[place.core, pl.ds(piece * STEP, STEP)]
        n = place.row_source(message)
        return pc.at[n // 2] if piece == COLS else rp.at[n, pl.ds(piece * STEP, STEP)]

    trees = {"R": R_TREES, "L": L_TREES, "S": S_TREES}
    receive = {"R": r_recv, "L": l_recv, "S": s_recv}
    number = {"R": 0, "L": 1, "S": 2}

    def start_one(name, message, piece, link, child, index):
        device = place.col_neighbour(link) if name == "L" else place.row_neighbour(link)
        sem = cols_send.at[number[name]] if piece is COLS else send.at[number[name]]
        to = ref_of(name, child, piece) if name == "S" else None
        remote(ref_of(name, message, piece), sem, receive[name].at[index, slot(child)], device, to).start()

    def send_on(name, message, piece):
        for link, child in trees[name][piece][message]:
            start_one(name, message, piece, link, child, piece)

    def arrive(name, message, piece):
        remote(
            ref_of(name, message, piece), send.at[number[name]], receive[name].at[piece, slot(message)], sibling
        ).wait_recv()
        send_on(name, message, piece)

    sib_sems = {"R": (r_sib, 3), "S": (s_sib, 4)}

    def chunk(name, message, core):
        if name == "S":
            return sp[slot(message)].at[core]
        return rp.at[place.row_source(message) // 2 * 2 + core]

    def to_sibling(name, message):
        sem, n = sib_sems[name]
        remote(chunk(name, message, place.core), send.at[n], sem.at[slot(message)], sibling).start()

    def from_sibling(name, message):
        sem, n = sib_sems[name]
        remote(chunk(name, message, 1 - place.core), send.at[n], sem.at[slot(message)], sibling).wait_recv()

    mine = pc.at[q, place.core]
    other = pc.at[q, 1 - place.core]
    remote(mine, cols_send.at[3], pair_sem.at[0], sibling).start()
    for k in range(PIECES):
        send_on("R", OWN, k)
        send_on("L", OWN, k)
    send_on("L", OWN, COLS)
    to_sibling("R", OWN)
    remote(other, cols_send.at[3], pair_sem.at[0], sibling).wait_recv()
    send_on("R", OWN, COLS)

    left = {m: PIECES for m in MESSAGES}
    for _, name, message, piece in plan([("R", R_TREES, R_LINKS), ("L", L_TREES, L_LINKS)]):
        arrive(name, message, piece)
        if name == "R" and piece != COLS:
            left[message] -= 1
            if left[message] == 0:
                to_sibling("R", message)

    copies = [
        pltpu.make_async_copy(pc, pc_s, local_sem.at[0]),
        pltpu.make_async_copy(lc, lc_s, local_sem.at[1]),
    ]
    for copy in copies:
        copy.start()
    for copy in copies:
        copy.wait()
    for message in MESSAGES:
        from_sibling("R", message)

    def wanted(i):
        js = [cs_ref[i * KC + s] for s in range(KC)]
        return [jnp.where(j >= 0, j, -2) for j in js]

    def split(v):
        hi = v.astype(jnp.bfloat16)
        return hi, (v - hi.astype(jnp.float32)).astype(jnp.bfloat16)

    def group_product(i, g, block, js):
        high, low = [], []
        for t in range(KC):
            m = jnp.maximum(lc_s[g, 0, i * KC + t], 0)
            core, row = m // ROWS % 2, m % ROWS
            held = [pc_s[g, core, 0, row * KC + u] for u in range(KC)]
            tiles = []
            for h in range(2):
                moved, found = [], []
                for s in (2 * h, 2 * h + 1):
                    j = js[s]
                    hit = [v == j for v in held]
                    half = jnp.where(hit[2] | hit[3], 1, 0)
                    odd = jnp.where(hit[1] | hit[3], 1, 0)
                    found.append(hit[0] | hit[1] | hit[2] | hit[3])
                    v = block(g, core, row, half)
                    shift = odd * 64 if s % 2 == 0 else 64 - odd * 64
                    moved.append(pltpu.roll(v, shift, 1))
                below = jnp.where(found[0], 64, 0)
                above = jnp.where(found[1], 64, 128)
                tiles.append(jnp.where(lane < below, moved[0], jnp.where(lane >= above, moved[1], 0.0)))
            hi, lo = split(jnp.concatenate(tiles, axis=1))
            high.append(hi)
            low.append(lo)
        w_hi = jnp.concatenate(high, axis=0)
        w_lo = jnp.concatenate(low, axis=0)
        a_hi, a_lo = split(jnp.concatenate([lp[g, i, 0], lp[g, i, 1]], axis=1))
        first = jnp.dot(jnp.concatenate([a_hi, a_lo], axis=0), w_hi, preferred_element_type=jnp.float32)
        second = jnp.dot(a_hi, w_lo, preferred_element_type=jnp.float32)
        return first[:64] + first[64:] + second

    def store_slots(out_ref, panel, i):
        for h in range(2):
            even = panel[h, pl.ds(0, 32, stride=2), :]
            odd = panel[h, pl.ds(1, 32, stride=2), :]
            out_ref[i, pl.ds(2 * h, 32, stride=4), :] = jnp.where(lane_half, even, pltpu.roll(odd, 64, 1))
            out_ref[i, pl.ds(2 * h + 1, 32, stride=4), :] = jnp.where(lane_half, pltpu.roll(even, 64, 1), odd)

    def square_piece(k, carry):
        def square_row(n, inner):
            i = k * STEP + n
            js = wanted(i)

            def add(g, total):
                return total + group_product(i, g, lambda g, core, row, half: rp[g * 2 + core, row, half], js)

            total = lax.fori_loop(0, N_C, add, jnp.zeros((64, 256), jnp.float32), unroll=8)
            sp[0][place.core, i, 0] = total[:, :128]
            sp[0][place.core, i, 1] = total[:, 128:]
            store_slots(sq_ref, sp[0].at[place.core, i], i)
            return inner

        lax.fori_loop(0, STEP, square_row, 0)
        for link, child in (("+", (1, 0)), ("-", (3, 0)), ("pair", (0, 1))):
            start_one("S", OWN, k, link, child, k)
        return carry

    lax.fori_loop(0, PIECES, square_piece, 0)
    to_sibling("S", OWN)

    def update_source(message, first):
        g = place.row_source(message) // 2
        panel = sp[slot(message)]

        def update_row(i, carry):
            total = group_product(i, g, lambda g, core, row, half: panel[core, row, half], wanted(i))
            if not first:
                total = total + jnp.concatenate([acc[i, 0], acc[i, 1]], axis=1)
            acc[i, 0] = total[:, :128]
            acc[i, 1] = total[:, 128:]
            return carry

        lax.fori_loop(0, ROWS, update_row, 0, unroll=2)

    events = [(t, "arrive", m, k) for t, _, m, k in plan([("S", S_TREES, R_LINKS)]) if k != COLS]
    done = {m: max(t for t, _, n, _ in events if n == m) for m in MESSAGES if m != OWN}
    done[OWN] = 0.0
    events += [(t, "share", m, 0) for m, t in done.items() if m != OWN]
    events += [(t + 4.0, "use", m, 0) for m, t in done.items()]
    used = 0
    for _, kind, message, piece in sorted(events, key=lambda e: e[0]):
        if kind == "arrive":
            arrive("S", message, piece)
        elif kind == "share":
            to_sibling("S", message)
        else:
            from_sibling("S", message)
            update_source(message, used == 0)
            used += 1

    def finish(i, carry):
        for h in range(2):
            acc[i, h] = 1.5 * rp[r, i, h] - 0.5 * acc[i, h]
        store_slots(up_ref, acc.at[i], i)
        return carry

    lax.fori_loop(0, ROWS, finish, 0)

    for name in ("R", "L", "S"):
        remote(rp.at[pl.ds(0, 7)], send.at[number[name]], receive[name].at[0, 0], sibling).wait_send()
    for name in ("R", "S"):
        sem, n = sib_sems[name]
        remote(rp.at[pl.ds(0, 8)], send.at[n], sem.at[0], sibling).wait_send()
    remote(pc.at[pl.ds(0, 7)], cols_send.at[0], r_recv.at[0, 0], sibling).wait_send()
    remote(lc.at[pl.ds(0, 7)], cols_send.at[1], l_recv.at[0, 0], sibling).wait_send()
    remote(mine, cols_send.at[3], pair_sem.at[0], sibling).wait_send()


def local(x_blocks, block_cols):
    x = x_blocks.reshape(ROWS, KC, 32, 128).transpose(0, 2, 1, 3).reshape(ROWS, 128, 128)
    flat = block_cols.reshape(ROWS * KC)
    tile = jnp.zeros((8, 128), jnp.int32).at[0, : ROWS * KC].set(flat)
    out = jax.ShapeDtypeStruct((ROWS, 128, 128), jnp.float32)
    vmem = pl.BlockSpec(memory_space=pltpu.VMEM)
    dma = pltpu.SemaphoreType.DMA
    square, updated = pl.pallas_call(
        kernel,
        out_shape=(out, out),
        in_specs=[vmem, vmem, pl.BlockSpec(memory_space=pltpu.SMEM)],
        out_specs=(vmem, vmem),
        scratch_shapes=[
            pltpu.VMEM((N_R, ROWS, 2, 64, 128), jnp.float32),
            pltpu.VMEM((N_C, ROWS, 2, 64, 128), jnp.float32),
            pltpu.VMEM((ROWS, 2, 64, 128), jnp.float32),
            pltpu.VMEM((N_R // 2, 2, 8, 128), jnp.int32),
            pltpu.VMEM((N_C, 8, 128), jnp.int32),
            pltpu.SMEM((N_R // 2, 2, 8, 128), jnp.int32),
            pltpu.SMEM((N_C, 8, 128), jnp.int32),
            dma((5,)),
            dma((4,)),
            dma((PIECES + 1, 8)),
            dma((PIECES + 1, 8)),
            dma((PIECES + 1, 8)),
            dma((8,)),
            dma((8,)),
            dma((1,)),
            dma((2,)),
        ]
        + [pltpu.VMEM((2, ROWS, 2, 64, 128), jnp.float32)] * 8,
        compiler_params=pltpu.CompilerParams(
            collective_id=0, has_side_effects=True, vmem_limit_bytes=56 << 20
        ),
        cost_estimate=pl.CostEstimate(flops=1 << 30, bytes_accessed=4 << 20, transcendentals=0),
    )(x, tile, flat)

    def back(y):
        return y.reshape(ROWS, 32, KC, 128).transpose(0, 2, 1, 3).reshape(ROWS, KC, 4096)

    return back(square), back(updated)


def solution(mesh):
    return jax.shard_map(
        local,
        mesh=mesh,
        in_specs=(P("row", "col", None), P("row", "col")),
        out_specs=(P("row", "col", None), P("row", "col", None)),
        check_vma=False,
    )
```

time: 772 us -> 207 us (0.27)
  local copies, waits for them, and re-layouts: 377 us -> 5.41 us
  waiting for transfers between devices: 238 us -> 0 us
  Pallas kernels: 0 us -> 200 us
  matrix products: 58.9 us -> 0 us
  blocking collectives: 48.1 us -> 0 us
  other arithmetic: 23.9 us -> 0 us
  between operations: 13.8 us -> 0.65 us
    gather x256 -> x0, local copies, waits for them, and re-layouts: 291 us -> none  [the longest x96 222 us: pick_blocks(): chosen = panel_vals[right_rows[:, None], where_u]]
    all_gather x3 -> x0, waiting for transfers between devices: 237 us -> none  [the longest x1 95.5 us: local(): square_vals = lax.all_gather(square, 'row', axis=0, tiled=True)]
    pallas_call x0 -> x1, Pallas kernels: none -> 200 us  [local(): pl.pallas_call(kernel, out_shape=(out, out), in_specs=[vmem, vmem, pl.Blo...]
    dot_general x32 -> x0, matrix products: 58.9 us -> none  [multiply_rows(): jnp.einsum('tab,tsbc->sac', left_vals.reshape(leading, BS, BS), chosen.re...]
    all_gather x2 -> x0, blocking collectives: 48.1 us -> none  [the longest x1 26.9 us: local(): lax.all_gather(block_cols, 'col', axis=1, tiled=True)]
    squeeze x64 -> x0, local copies, waits for them, and re-layouts: 35 us -> none  [panel_product(): return lax.map(one_row, (row_vals, row_cols, own_cols))]
    dynamic_update_slice x32 -> x0, local copies, waits for them, and re-layouts: 20.4 us -> none  [panel_product(): return lax.map(one_row, (row_vals, row_cols, own_cols))]
    while x3 -> x0, local copies, waits for them, and re-layouts: 12 us -> none  [panel_product(): return lax.map(one_row, (row_vals, row_cols, own_cols))]
  transfers between devices with their start and end apart: 3 -> 0, of which waited for: 3 -> 0; matrix products, arithmetic and copies ran while one was open for 2% -> 0% of each run, Pallas kernels for 0% -> 0%
where the time goes in v1:
time: 207 us; the launch traced here: 206 us
  Pallas kernels  200 us (97%)
  local copies, waits for them, and re-layouts  5.41 us (3%)
    pallas_call x1, Pallas kernels, local(): pl.pallas_call(kernel, out_shape=(out, out), in_specs=[vmem, vmem, pl.Blo...  200 us

profile of v1, /device:TPU:1, one launch (start us, length us, event | category | flops | bytes accessed | tf_op | source)
XLA Modules:
  0.0 206.2 jit_solution(18000042786897630639)
XLA Ops:
  0.6 0.8 copy.10
  1.4 0.6 reshape.60.cs_ref
  2.0 0.1 reshape.59
  2.1 0.6 scatter.4.tile_ref
  2.7 200.1 %shard_map.41 = (f32[16,128,128]{2,1,0:T(8,128)}, f32[16,128,128]{2,1,0:T(8,128)}) custom-call(f32[16,128,128]{2,1,0:T(8,128)} %bitcast.17, s32[8,128]{1,0:T(8,128)} %scatter.4.tile_ref, s32[64]{0:T(128)} %reshape.60.cs_ref), custom_call_target="tpu_custom_call" | custom-call | flops 1073741824 | bytes 4194304 | tf_op jit(solution)/shard_map/pallas_call | solution.py:367
  202.8 0.0 copy-start
  202.8 2.4 %copy.16 = f32[16,4,4096]{2,1,0:T(4,128)} copy(f32[16,4,4096]{2,1,0:T(4,128)} %bitcast.16) | data formatting | bytes 2097152
  205.2 0.0 copy-done
  205.2 1.0 copy.17
Async XLA Ops:
  202.8 2.4 %copy-start = (f32[16,128,128]{2,1,0:T(8,128)S(1)}, f32[16,128,128]{2,1,0:T(8,128)}, u32[]{:S(2)}) copy-start(f32[16,128,128]{2,1,0:T(8,128)} %get-tuple-element.17) | copy-start | bytes 3145732

commit v2 on v1

--- a/solution.py
+++ b/solution.py
@@ -17,6 +17,10 @@
 STEP = ROWS // PIECES
 PIECE_US = 23.0 / PIECES
 HOP_US = 1.5
+R_GAP, L_GAP, S_GAP = 3.0, 8.0, 2.0
+CHUNK = 2 * ROWS
+SPAN = 2 * CHUNK + 1
+ZERO = 2 * CHUNK
 COLS = PIECES
 
 OWN = (0, 0)
@@ -52,15 +56,14 @@
     order = []
     queue = []
     count = 0
-    for name, trees, links in gathers:
+    for name, trees, links, gap in gathers:
         for piece in [COLS] + list(range(PIECES)):
             count += 1
-            heapq.heappush(queue, (0.01 * (piece + 1) if piece != COLS else 0.0, count, name, OWN, piece))
-    table = {name: (trees, links) for name, trees, links in gathers}
+            heapq.heappush(queue, (gap * piece if piece != COLS else 0.0, count, name, OWN, piece))
+    table = {name: (trees, links) for name, trees, links, _ in gathers}
     while queue:
         now, _, name, message, piece = heapq.heappop(queue)
-        if message != OWN:
-            order.append((now, name, message, piece))
+        order.append((now, name, message, piece))
         trees, links = table[name]
         for link, child in trees[piece][message]:
             wire = links[link]
@@ -133,7 +136,7 @@
 
 def kernel(
     x_ref, tile_ref, cs_ref, sq_ref, up_ref,
-    rp, lp, acc, pc, lc, pc_s, lc_s,
+    rp, lp, acc, pc, lc, pc_s, lc_s, at_s, low_s, high_s,
     send, cols_send, r_recv, l_recv, s_recv, r_sib, s_sib, pair_sem, local_sem,
     *sp,
 ):
@@ -142,6 +145,7 @@
     sibling = place.sibling()
     lane = lax.broadcasted_iota(jnp.int32, (64, 128), 1)
     lane_half = lax.broadcasted_iota(jnp.int32, (32, 128), 1) < 64
+    home = q * SPAN + place.core * CHUNK
 
     barrier = pltpu.get_barrier_semaphore()
     neighbours = [place.row_neighbour(k) for k in ("+", "-", "pair")]
@@ -157,24 +161,33 @@
                 pair.append(jnp.where(cs_ref[i * KC + u] >= 0, v, 0.0))
             even = jnp.where(lane_half, pair[0], pltpu.roll(pair[1], 64, 1))
             odd = jnp.where(lane_half, pltpu.roll(pair[0], 64, 1), pair[1])
-            for panel, n in ((rp, r), (lp, c)):
-                panel[n, i, h, pl.ds(0, 32, stride=2), :] = even
-                panel[n, i, h, pl.ds(1, 32, stride=2), :] = odd
+            for n, part in enumerate((even, odd)):
+                rp[home + 2 * i + h, pl.ds(n, 32, stride=2), :] = part
+                lp[c, i, h, pl.ds(n, 32, stride=2), :] = part
         return carry
 
     lax.fori_loop(0, ROWS, convert, 0)
+    for n in range(8):
+        rp[n * SPAN + ZERO] = jnp.zeros((64, 128), jnp.float32)
+        sp[n][ZERO] = jnp.zeros((64, 128), jnp.float32)
     pc[q, place.core] = tile_ref[...]
     lc[c] = tile_ref[...]
     pl.semaphore_wait(barrier, len(neighbours))
 
-    def ref_of(name, message, piece):
+    def ref_of(name, message, piece, core=None):
         if name == "L":
             n = place.col_source(message)
             return lc.at[n] if piece == COLS else lp.at[n, pl.ds(piece * STEP, STEP)]
+        first = (place.core if core is None else core) * CHUNK
+        chip = place.row_source(message) // 2
+        if name == "R" and piece == COLS:
+            return pc.at[chip]
+        n = CHUNK
+        if piece is not None:
+            first, n = first + piece * 2 * STEP, 2 * STEP
         if name == "S":
-            return sp[slot(message)].at[place.core, pl.ds(piece * STEP, STEP)]
-        n = place.row_source(message)
-        return pc.at[n // 2] if piece == COLS else rp.at[n, pl.ds(piece * STEP, STEP)]
+            return sp[slot(message)].at[pl.ds(first, n)]
+        return rp.at[pl.ds(chip * SPAN + first, n)]
 
     trees = {"R": R_TREES, "L": L_TREES, "S": S_TREES}
     receive = {"R": r_recv, "L": l_recv, "S": s_recv}
@@ -195,81 +208,110 @@
             ref_of(name, message, piece), send.at[number[name]], receive[name].at[piece, slot(message)], sibling
         ).wait_recv()
         send_on(name, message, piece)
+        if name != "L" and piece != COLS:
+            to_sibling(name, message, piece)
 
     sib_sems = {"R": (r_sib, 3), "S": (s_sib, 4)}
 
-    def chunk(name, message, core):
-        if name == "S":
-            return sp[slot(message)].at[core]
-        return rp.at[place.row_source(message) // 2 * 2 + core]
-
-    def to_sibling(name, message):
+    def to_sibling(name, message, piece):
         sem, n = sib_sems[name]
-        remote(chunk(name, message, place.core), send.at[n], sem.at[slot(message)], sibling).start()
+        remote(ref_of(name, message, piece), send.at[n], sem.at[slot(message)], sibling).start()
 
     def from_sibling(name, message):
         sem, n = sib_sems[name]
-        remote(chunk(name, message, 1 - place.core), send.at[n], sem.at[slot(message)], sibling).wait_recv()
+        whole = ref_of(name, message, None, 1 - place.core)
+        remote(whole, send.at[n], sem.at[slot(message)], sibling).wait_recv()
 
     mine = pc.at[q, place.core]
     other = pc.at[q, 1 - place.core]
     remote(mine, cols_send.at[3], pair_sem.at[0], sibling).start()
-    for k in range(PIECES):
-        send_on("R", OWN, k)
-        send_on("L", OWN, k)
     send_on("L", OWN, COLS)
-    to_sibling("R", OWN)
     remote(other, cols_send.at[3], pair_sem.at[0], sibling).wait_recv()
     send_on("R", OWN, COLS)
 
-    left = {m: PIECES for m in MESSAGES}
-    for _, name, message, piece in plan([("R", R_TREES, R_LINKS), ("L", L_TREES, L_LINKS)]):
-        arrive(name, message, piece)
-        if name == "R" and piece != COLS:
-            left[message] -= 1
-            if left[message] == 0:
-                to_sibling("R", message)
-
-    copies = [
-        pltpu.make_async_copy(pc, pc_s, local_sem.at[0]),
-        pltpu.make_async_copy(lc, lc_s, local_sem.at[1]),
+    def load_columns():
+        copies = [
+            pltpu.make_async_copy(pc, pc_s, local_sem.at[0]),
+            pltpu.make_async_copy(lc, lc_s, local_sem.at[1]),
+        ]
+        for copy in copies:
+            copy.start()
+        for copy in copies:
+            copy.wait()
+
+    def find_row(i, carry):
+        js = [cs_ref[i * KC + s] for s in range(KC)]
+        js = [jnp.where(j >= 0, j, -2) for j in js]
+
+        def find(n, inner):
+            m = lc_s[n // KC, 0, i * KC + n % KC]
+            there = jnp.maximum(m, 0)
+            core, row = there // ROWS % 2, there % ROWS
+            held = [pc_s[n // KC, core, 0, row * KC + u] for u in range(KC)]
+            start = (core * ROWS + row) * 2
+            spot = i * 32 + n
+            for s in range(KC):
+                hit = [v == js[s] for v in held]
+                at = jnp.where(hit[0] | hit[1], start, jnp.where(hit[2] | hit[3], start + 1, ZERO))
+                at_s[spot * KC + s] = jnp.where(m >= 0, at, ZERO)
+                odd = hit[1] | hit[3]
+                if s % 2 == 0:
+                    low_s[spot * 2 + s // 2] = jnp.where(odd, 64, 0)
+                else:
+                    high_s[spot * 2 + s // 2] = jnp.where(odd, 128, 64)
+            return inner
+
+        return lax.fori_loop(0, 32, find, carry, unroll=4)
+
+    def find_rows(n):
+        lax.fori_loop(n * 4, n * 4 + 4, find_row, 0)
+
+    events = [
+        (t, name, m, k)
+        for t, name, m, k in plan([("R", R_TREES, R_LINKS, R_GAP), ("L", L_TREES, L_LINKS, L_GAP)])
+        if not (m == OWN and k == COLS)
     ]
-    for copy in copies:
-        copy.start()
-    for copy in copies:
-        copy.wait()
+    known = max(t for t, _, _, k in events if k == COLS)
+    events += [(known + 0.1 + 4.0 * n, "find", None, n) for n in range(4)]
+    events.sort(key=lambda e: e[0])
+    ready = max(t for t, name, _, _ in events if name != "L")
+
+    def follow(some):
+        for _, name, message, piece in some:
+            if name == "find":
+                if piece == 0:
+                    load_columns()
+                find_rows(piece)
+            elif message == OWN:
+                send_on(name, message, piece)
+                if name == "R":
+                    to_sibling(name, message, piece)
+            else:
+                arrive(name, message, piece)
+
+    follow([e for e in events if e[0] <= ready])
+    late = [e for e in events if e[0] > ready]
     for message in MESSAGES:
         from_sibling("R", message)
-
-    def wanted(i):
-        js = [cs_ref[i * KC + s] for s in range(KC)]
-        return [jnp.where(j >= 0, j, -2) for j in js]
 
     def split(v):
         hi = v.astype(jnp.bfloat16)
         return hi, (v - hi.astype(jnp.float32)).astype(jnp.bfloat16)
 
-    def group_product(i, g, block, js):
+    left_half = lane < 64
+
+    def group_product(i, g, block):
         high, low = [], []
         for t in range(KC):
-            m = jnp.maximum(lc_s[g, 0, i * KC + t], 0)
-            core, row = m // ROWS % 2, m % ROWS
-            held = [pc_s[g, core, 0, row * KC + u] for u in range(KC)]
+            spot = i * 32 + g * KC + t
             tiles = []
             for h in range(2):
-                moved, found = [], []
-                for s in (2 * h, 2 * h + 1):
-                    j = js[s]
-                    hit = [v == j for v in held]
-                    half = jnp.where(hit[2] | hit[3], 1, 0)
-                    odd = jnp.where(hit[1] | hit[3], 1, 0)
-                    found.append(hit[0] | hit[1] | hit[2] | hit[3])
-                    v = block(g, core, row, half)
-                    shift = odd * 64 if s % 2 == 0 else 64 - odd * 64
-                    moved.append(pltpu.roll(v, shift, 1))
-                below = jnp.where(found[0], 64, 0)
-                above = jnp.where(found[1], 64, 128)
-                tiles.append(jnp.where(lane < below, moved[0], jnp.where(lane >= above, moved[1], 0.0)))
+                one = block(at_s[spot * KC + 2 * h])
+                two = block(at_s[spot * KC + 2 * h + 1])
+                kept = (lane >= low_s[spot * 2 + h]) & (lane < high_s[spot * 2 + h])
+                straight = jnp.where(left_half, one, two)
+                swapped = pltpu.roll(jnp.where(left_half, two, one), 64, 1)
+                tiles.append(jnp.where(kept, straight, swapped))
             hi, lo = split(jnp.concatenate(tiles, axis=1))
             high.append(hi)
             low.append(lo)
@@ -280,60 +322,63 @@
         second = jnp.dot(a_hi, w_lo, preferred_element_type=jnp.float32)
         return first[:64] + first[64:] + second
 
-    def store_slots(out_ref, panel, i):
+    def store_slots(out_ref, i, read):
         for h in range(2):
-            even = panel[h, pl.ds(0, 32, stride=2), :]
-            odd = panel[h, pl.ds(1, 32, stride=2), :]
+            even = read(h, pl.ds(0, 32, stride=2))
+            odd = read(h, pl.ds(1, 32, stride=2))
             out_ref[i, pl.ds(2 * h, 32, stride=4), :] = jnp.where(lane_half, even, pltpu.roll(odd, 64, 1))
             out_ref[i, pl.ds(2 * h + 1, 32, stride=4), :] = jnp.where(lane_half, pltpu.roll(even, 64, 1), odd)
 
     def square_piece(k, carry):
         def square_row(n, inner):
             i = k * STEP + n
-            js = wanted(i)
 
             def add(g, total):
-                return total + group_product(i, g, lambda g, core, row, half: rp[g * 2 + core, row, half], js)
+                return total + group_product(i, g, lambda at: rp[g * SPAN + at])
 
             total = lax.fori_loop(0, N_C, add, jnp.zeros((64, 256), jnp.float32), unroll=8)
-            sp[0][place.core, i, 0] = total[:, :128]
-            sp[0][place.core, i, 1] = total[:, 128:]
-            store_slots(sq_ref, sp[0].at[place.core, i], i)
+            spot = place.core * CHUNK + 2 * i
+            sp[0][spot] = total[:, :128]
+            sp[0][spot + 1] = total[:, 128:]
+            store_slots(sq_ref, i, lambda h, rows: sp[0][spot + h, rows, :])
             return inner
 
         lax.fori_loop(0, STEP, square_row, 0)
         for link, child in (("+", (1, 0)), ("-", (3, 0)), ("pair", (0, 1))):
             start_one("S", OWN, k, link, child, k)
+        to_sibling("S", OWN, k)
         return carry
 
-    lax.fori_loop(0, PIECES, square_piece, 0)
-    to_sibling("S", OWN)
+    full = min([PIECES] + [k for _, _, _, k in late])
+    lax.fori_loop(0, full, square_piece, 0)
+    for k in range(full, PIECES):
+        needed = [n for n, e in enumerate(late) if e[3] <= k]
+        if needed:
+            follow(late[: needed[-1] + 1])
+            late = late[needed[-1] + 1 :]
+        square_piece(k, 0)
 
     def update_source(message, first):
         g = place.row_source(message) // 2
         panel = sp[slot(message)]
 
         def update_row(i, carry):
-            total = group_product(i, g, lambda g, core, row, half: panel[core, row, half], wanted(i))
+            total = group_product(i, g, lambda at: panel[at])
             if not first:
                 total = total + jnp.concatenate([acc[i, 0], acc[i, 1]], axis=1)
             acc[i, 0] = total[:, :128]
             acc[i, 1] = total[:, 128:]
             return carry
 
-        lax.fori_loop(0, ROWS, update_row, 0, unroll=2)
-
-    events = [(t, "arrive", m, k) for t, _, m, k in plan([("S", S_TREES, R_LINKS)]) if k != COLS]
+        lax.fori_loop(0, ROWS, update_row, 0, unroll=4)
+
+    events = [(t, "arrive", m, k) for t, _, m, k in plan([("S", S_TREES, R_LINKS, S_GAP)]) if k != COLS and m != OWN]
     done = {m: max(t for t, _, n, _ in events if n == m) for m in MESSAGES if m != OWN}
-    done[OWN] = 0.0
-    events += [(t, "share", m, 0) for m, t in done.items() if m != OWN]
-    events += [(t + 4.0, "use", m, 0) for m, t in done.items()]
+    events += [(t + 1.5, "use", m, 0) for m, t in done.items()] + [(2.0, "use", OWN, 0)]
     used = 0
     for _, kind, message, piece in sorted(events, key=lambda e: e[0]):
         if kind == "arrive":
             arrive("S", message, piece)
-        elif kind == "share":
-            to_sibling("S", message)
         else:
             from_sibling("S", message)
             update_source(message, used == 0)
@@ -341,17 +386,17 @@
 
     def finish(i, carry):
         for h in range(2):
-            acc[i, h] = 1.5 * rp[r, i, h] - 0.5 * acc[i, h]
-        store_slots(up_ref, acc.at[i], i)
+            acc[i, h] = 1.5 * rp[home + 2 * i + h] - 0.5 * acc[i, h]
+        store_slots(up_ref, i, lambda h, rows: acc[i, h, rows, :])
         return carry
 
     lax.fori_loop(0, ROWS, finish, 0)
 
     for name in ("R", "L", "S"):
-        remote(rp.at[pl.ds(0, 7)], send.at[number[name]], receive[name].at[0, 0], sibling).wait_send()
+        remote(rp.at[pl.ds(0, 7 * CHUNK)], send.at[number[name]], receive[name].at[0, 0], sibling).wait_send()
     for name in ("R", "S"):
         sem, n = sib_sems[name]
-        remote(rp.at[pl.ds(0, 8)], send.at[n], sem.at[0], sibling).wait_send()
+        remote(rp.at[pl.ds(0, 8 * CHUNK)], send.at[n], sem.at[0], sibling).wait_send()
     remote(pc.at[pl.ds(0, 7)], cols_send.at[0], r_recv.at[0, 0], sibling).wait_send()
     remote(lc.at[pl.ds(0, 7)], cols_send.at[1], l_recv.at[0, 0], sibling).wait_send()
     remote(mine, cols_send.at[3], pair_sem.at[0], sibling).wait_send()
@@ -370,13 +415,16 @@
         in_specs=[vmem, vmem, pl.BlockSpec(memory_space=pltpu.SMEM)],
         out_specs=(vmem, vmem),
         scratch_shapes=[
-            pltpu.VMEM((N_R, ROWS, 2, 64, 128), jnp.float32),
+            pltpu.VMEM((N_R // 2 * SPAN, 64, 128), jnp.float32),
             pltpu.VMEM((N_C, ROWS, 2, 64, 128), jnp.float32),
             pltpu.VMEM((ROWS, 2, 64, 128), jnp.float32),
             pltpu.VMEM((N_R // 2, 2, 8, 128), jnp.int32),
             pltpu.VMEM((N_C, 8, 128), jnp.int32),
             pltpu.SMEM((N_R // 2, 2, 8, 128), jnp.int32),
             pltpu.SMEM((N_C, 8, 128), jnp.int32),
+            pltpu.SMEM((ROWS * 32 * KC,), jnp.int32),
+            pltpu.SMEM((ROWS * 32 * 2,), jnp.int32),
+            pltpu.SMEM((ROWS * 32 * 2,), jnp.int32),
             dma((5,)),
             dma((4,)),
             dma((PIECES + 1, 8)),
@@ -387,7 +435,7 @@
             dma((1,)),
             dma((2,)),
         ]
-        + [pltpu.VMEM((2, ROWS, 2, 64, 128), jnp.float32)] * 8,
+        + [pltpu.VMEM((SPAN, 64, 128), jnp.float32)] * 8,
         compiler_params=pltpu.CompilerParams(
             collective_id=0, has_side_effects=True, vmem_limit_bytes=56 << 20
         ),

time: 207 us -> 169 us (0.82)
  Pallas kernels: 200 us -> 163 us
    pallas_call x1, Pallas kernels: 200 us -> 163 us  [local(): pl.pallas_call(kernel, out_shape=(out, out), in_specs=[vmem, vmem, pl.Blo...]
where the time goes in v2:
time: 169 us
  Pallas kernels  163 us (96%)
  local copies, waits for them, and re-layouts  5.41 us (3%)
    pallas_call x1, Pallas kernels, local(): pl.pallas_call(kernel, out_shape=(out, out), in_specs=[vmem, vmem, pl.Blo...  163 us
    unnamed x5, local copies, waits for them, and re-layouts  4.12 us

profile of v2, /device:TPU:1, one launch (start us, length us, event | category | flops | bytes accessed | tf_op | source)
XLA Modules:
  0.0 168.9 jit_solution(3665391551548910278)
XLA Ops:
  0.6 0.8 copy.10
  1.4 0.6 reshape.60.cs_ref
  2.0 0.1 reshape.59
  2.1 0.6 scatter.4.tile_ref
  2.7 162.9 %shard_map.41 = (f32[16,128,128]{2,1,0:T(8,128)}, f32[16,128,128]{2,1,0:T(8,128)}) custom-call(f32[16,128,128]{2,1,0:T(8,128)} %bitcast.17, s32[8,128]{1,0:T(8,128)} %scatter.4.tile_ref, s32[64]{0:T(128)} %reshape.60.cs_ref), custom_call_target="tpu_custom_call" | custom-call | flops 1073741824 | bytes 4194304 | tf_op jit(solution)/shard_map/pallas_call | solution.py:412
  165.6 0.0 copy-start
  165.6 2.4 %copy.16 = f32[16,4,4096]{2,1,0:T(4,128)} copy(f32[16,4,4096]{2,1,0:T(4,128)} %bitcast.16) | data formatting | bytes 2097152
  168.0 0.0 copy-done
  168.0 1.0 copy.17
Async XLA Ops:
  165.6 2.4 %copy-start = (f32[16,128,128]{2,1,0:T(8,128)S(1)}, f32[16,128,128]{2,1,0:T(8,128)}, u32[]{:S(2)}) copy-start(f32[16,128,128]{2,1,0:T(8,128)} %get-tuple-element.17) | copy-start | bytes 3145732

commit v3 on v2

--- a/solution.py
+++ b/solution.py
@@ -17,10 +17,14 @@
 STEP = ROWS // PIECES
 PIECE_US = 23.0 / PIECES
 HOP_US = 1.5
-R_GAP, L_GAP, S_GAP = 3.0, 8.0, 2.0
+FIND_GAP = 2.5
+SQUARE_US = 1.1
+R_GAP, L_GAP = 3.0, 6.0
 CHUNK = 2 * ROWS
 SPAN = 2 * CHUNK + 1
 ZERO = 2 * CHUNK
+TOGETHER = 4
+GROUP = 4
 COLS = PIECES
 
 OWN = (0, 0)
@@ -56,10 +60,10 @@
     order = []
     queue = []
     count = 0
-    for name, trees, links, gap in gathers:
+    for name, trees, links, starts in gathers:
         for piece in [COLS] + list(range(PIECES)):
             count += 1
-            heapq.heappush(queue, (gap * piece if piece != COLS else 0.0, count, name, OWN, piece))
+            heapq.heappush(queue, (starts[piece] if piece != COLS else 0.0, count, name, OWN, piece))
     table = {name: (trees, links) for name, trees, links, _ in gathers}
     while queue:
         now, _, name, message, piece = heapq.heappop(queue)
@@ -78,11 +82,43 @@
     return [tree(k, pair_first[k]) for k in range(PIECES)] + [tree(0, True)]
 
 
-R_TREES = trees_of([k % 4 != 3 for k in range(PIECES)])
+R_TREES = trees_of([k not in (2, 3) for k in range(PIECES)])
 L_TREES = trees_of([True] * PIECES)
 S_TREES = trees_of([k % 8 not in (2, 5, 7) for k in range(PIECES)])
 R_LINKS = {"+": "x+", "-": "x-", "pair": "y"}
 L_LINKS = {"+": "z+", "-": "z-", "pair": "y"}
+
+
+def whole_plan():
+    first = [
+        ("R", R_TREES, R_LINKS, [R_GAP * k for k in range(PIECES)]),
+        ("L", L_TREES, L_LINKS, [L_GAP * k for k in range(PIECES)]),
+    ]
+    steps = plan(first)
+    ready = max(t for t, name, _, _ in steps if name == "R")
+    starts, now = [], ready + 2.0
+    for k in range(PIECES):
+        now = max(now, max(t for t, name, _, n in steps if name == "L" and n <= k) + 0.5) + SQUARE_US
+        starts.append(now)
+    steps = plan(first + [("S", S_TREES, R_LINKS, starts)])
+    known = max(t for t, name, _, n in steps if name != "S" and n == COLS)
+    events = [(known + 0.1 + FIND_GAP * n, "find", "", None, n) for n in range(ROWS)]
+    done = {}
+    for t, name, message, piece in steps:
+        if name == "S" and piece == COLS or message == OWN and name != "S" and piece in (COLS, 0):
+            continue
+        if message != OWN:
+            events.append((t, "arrive", name, message, piece))
+            if name == "S":
+                done[message] = max(t, done.get(message, 0.0))
+        elif name == "S":
+            events.append((t - SQUARE_US, "square", name, message, piece))
+        else:
+            events.append((t, "send", name, message, piece))
+    events += [(t + 1.5, "use", "S", message, 0) for message, t in done.items()]
+    events.append((starts[-1] + 0.1, "use", "S", OWN, 0))
+    events.sort(key=lambda e: e[0])
+    return [e[1:] for e in events]
 
 
 class Place:
@@ -135,7 +171,7 @@
 
 
 def kernel(
-    x_ref, tile_ref, cs_ref, sq_ref, up_ref,
+    x_ref, cols_ref, cs_ref, sq_ref, up_ref,
     rp, lp, acc, pc, lc, pc_s, lc_s, at_s, low_s, high_s,
     send, cols_send, r_recv, l_recv, s_recv, r_sib, s_sib, pair_sem, local_sem,
     *sp,
@@ -158,7 +194,7 @@
             pair = []
             for u in (2 * h, 2 * h + 1):
                 v = x_ref[i, pl.ds(u, 32, stride=4), :]
-                pair.append(jnp.where(cs_ref[i * KC + u] >= 0, v, 0.0))
+                pair.append(jnp.where(cs_ref[u, i] >= 0, v, 0.0))
             even = jnp.where(lane_half, pair[0], pltpu.roll(pair[1], 64, 1))
             odd = jnp.where(lane_half, pltpu.roll(pair[0], 64, 1), pair[1])
             for n, part in enumerate((even, odd)):
@@ -170,8 +206,9 @@
     for n in range(8):
         rp[n * SPAN + ZERO] = jnp.zeros((64, 128), jnp.float32)
         sp[n][ZERO] = jnp.zeros((64, 128), jnp.float32)
-    pc[q, place.core] = tile_ref[...]
-    lc[c] = tile_ref[...]
+    for tile in (pc.at[q, place.core], lc.at[c]):
+        tile[...] = jnp.zeros((8, 128), jnp.int32)
+        tile[:KC, :ROWS] = cols_ref[...]
     pl.semaphore_wait(barrier, len(neighbours))
 
     def ref_of(name, message, piece, core=None):
@@ -226,6 +263,9 @@
     other = pc.at[q, 1 - place.core]
     remote(mine, cols_send.at[3], pair_sem.at[0], sibling).start()
     send_on("L", OWN, COLS)
+    send_on("R", OWN, 0)
+    send_on("L", OWN, 0)
+    to_sibling("R", OWN, 0)
     remote(other, cols_send.at[3], pair_sem.at[0], sibling).wait_recv()
     send_on("R", OWN, COLS)
 
@@ -240,14 +280,14 @@
             copy.wait()
 
     def find_row(i, carry):
-        js = [cs_ref[i * KC + s] for s in range(KC)]
+        js = [cs_ref[s, i] for s in range(KC)]
         js = [jnp.where(j >= 0, j, -2) for j in js]
 
         def find(n, inner):
-            m = lc_s[n // KC, 0, i * KC + n % KC]
+            m = lc_s[n // KC, n % KC, i]
             there = jnp.maximum(m, 0)
             core, row = there // ROWS % 2, there % ROWS
-            held = [pc_s[n // KC, core, 0, row * KC + u] for u in range(KC)]
+            held = [pc_s[n // KC, core, u, row] for u in range(KC)]
             start = (core * ROWS + row) * 2
             spot = i * 32 + n
             for s in range(KC):
@@ -262,37 +302,6 @@
             return inner
 
         return lax.fori_loop(0, 32, find, carry, unroll=4)
-
-    def find_rows(n):
-        lax.fori_loop(n * 4, n * 4 + 4, find_row, 0)
-
-    events = [
-        (t, name, m, k)
-        for t, name, m, k in plan([("R", R_TREES, R_LINKS, R_GAP), ("L", L_TREES, L_LINKS, L_GAP)])
-        if not (m == OWN and k == COLS)
-    ]
-    known = max(t for t, _, _, k in events if k == COLS)
-    events += [(known + 0.1 + 4.0 * n, "find", None, n) for n in range(4)]
-    events.sort(key=lambda e: e[0])
-    ready = max(t for t, name, _, _ in events if name != "L")
-
-    def follow(some):
-        for _, name, message, piece in some:
-            if name == "find":
-                if piece == 0:
-                    load_columns()
-                find_rows(piece)
-            elif message == OWN:
-                send_on(name, message, piece)
-                if name == "R":
-                    to_sibling(name, message, piece)
-            else:
-                arrive(name, message, piece)
-
-    follow([e for e in events if e[0] <= ready])
-    late = [e for e in events if e[0] > ready]
-    for message in MESSAGES:
-        from_sibling("R", message)
 
     def split(v):
         hi = v.astype(jnp.bfloat16)
@@ -349,48 +358,59 @@
         to_sibling("S", OWN, k)
         return carry
 
-    full = min([PIECES] + [k for _, _, _, k in late])
-    lax.fori_loop(0, full, square_piece, 0)
-    for k in range(full, PIECES):
-        needed = [n for n, e in enumerate(late) if e[3] <= k]
-        if needed:
-            follow(late[: needed[-1] + 1])
-            late = late[needed[-1] + 1 :]
-        square_piece(k, 0)
-
-    def update_source(message, first):
+    def update_source(message, first, last):
         g = place.row_source(message) // 2
         panel = sp[slot(message)]
 
-        def update_row(i, carry):
-            total = group_product(i, g, lambda at: panel[at])
-            if not first:
-                total = total + jnp.concatenate([acc[i, 0], acc[i, 1]], axis=1)
-            acc[i, 0] = total[:, :128]
-            acc[i, 1] = total[:, 128:]
+        def update_rows(n, carry):
+            rows = [n * GROUP + i for i in range(GROUP)]
+            totals = [group_product(i, g, lambda at: panel[at]) for i in rows]
+            for i, total in zip(rows, totals):
+                for h in range(2):
+                    half = total[:, h * 128 : h * 128 + 128]
+                    if not first:
+                        half = half + acc[i, h]
+                    if last:
+                        half = 1.5 * rp[home + 2 * i + h] - 0.5 * half
+                    acc[i, h] = half
+                if last:
+                    store_slots(up_ref, i, lambda h, rows: acc[i, h, rows, :])
             return carry
 
-        lax.fori_loop(0, ROWS, update_row, 0, unroll=4)
-
-    events = [(t, "arrive", m, k) for t, _, m, k in plan([("S", S_TREES, R_LINKS, S_GAP)]) if k != COLS and m != OWN]
-    done = {m: max(t for t, _, n, _ in events if n == m) for m in MESSAGES if m != OWN}
-    events += [(t + 1.5, "use", m, 0) for m, t in done.items()] + [(2.0, "use", OWN, 0)]
-    used = 0
-    for _, kind, message, piece in sorted(events, key=lambda e: e[0]):
-        if kind == "arrive":
-            arrive("S", message, piece)
-        else:
+        lax.fori_loop(0, ROWS // GROUP, update_rows, 0)
+
+    def follow(event):
+        kind, name, message, piece = event
+        if kind == "find":
+            if piece == 0:
+                load_columns()
+            find_row(piece, 0)
+        elif kind == "send":
+            send_on(name, message, piece)
+            if name == "R":
+                to_sibling(name, message, piece)
+        elif kind == "arrive":
+            arrive(name, message, piece)
+        elif kind == "use":
             from_sibling("S", message)
-            update_source(message, used == 0)
-            used += 1
-
-    def finish(i, carry):
-        for h in range(2):
-            acc[i, h] = 1.5 * rp[home + 2 * i + h] - 0.5 * acc[i, h]
-        store_slots(up_ref, i, lambda h, rows: acc[i, h, rows, :])
-        return carry
-
-    lax.fori_loop(0, ROWS, finish, 0)
+            update_source(message, not used, len(used) == 7)
+            used.append(message)
+        elif piece == 0:
+            for m in MESSAGES:
+                from_sibling("R", m)
+            lax.fori_loop(0, TOGETHER, square_piece, 0)
+        elif piece >= TOGETHER:
+            square_piece(piece, 0)
+
+    used = []
+    events = whole_plan()
+    while events:
+        if events[0][0] == "square":
+            limit = TOGETHER - 1 if events[0][3] == 0 else events[0][3]
+            for event in [e for e in events if e[0] in ("find", "send") or e[1] == "L" and e[3] <= limit]:
+                events.remove(event)
+                follow(event)
+        follow(events.pop(0))
 
     for name in ("R", "L", "S"):
         remote(rp.at[pl.ds(0, 7 * CHUNK)], send.at[number[name]], receive[name].at[0, 0], sibling).wait_send()
@@ -404,8 +424,7 @@
 
 def local(x_blocks, block_cols):
     x = x_blocks.reshape(ROWS, KC, 32, 128).transpose(0, 2, 1, 3).reshape(ROWS, 128, 128)
-    flat = block_cols.reshape(ROWS * KC)
-    tile = jnp.zeros((8, 128), jnp.int32).at[0, : ROWS * KC].set(flat)
+    cols = block_cols.T
     out = jax.ShapeDtypeStruct((ROWS, 128, 128), jnp.float32)
     vmem = pl.BlockSpec(memory_space=pltpu.VMEM)
     dma = pltpu.SemaphoreType.DMA
@@ -440,7 +459,7 @@
             collective_id=0, has_side_effects=True, vmem_limit_bytes=56 << 20
         ),
         cost_estimate=pl.CostEstimate(flops=1 << 30, bytes_accessed=4 << 20, transcendentals=0),
-    )(x, tile, flat)
+    )(x, cols, cols)
 
     def back(y):
         return y.reshape(ROWS, 32, KC, 128).transpose(0, 2, 1, 3).reshape(ROWS, KC, 4096)

time: 169 us -> 152 us (0.90)
  Pallas kernels: 163 us -> 148 us
  local copies, waits for them, and re-layouts: 5.41 us -> 3.36 us
    pallas_call x1, Pallas kernels: 163 us -> 148 us  [local(): pl.pallas_call(kernel, out_shape=(out, out), in_specs=[vmem, vmem, pl.Blo...]
    unnamed x5 -> x4, local copies, waits for them, and re-layouts: 4.12 us -> 3.36 us
where the time goes in v3:
time: 152 us
  Pallas kernels  148 us (97%)
  local copies, waits for them, and re-layouts  3.36 us (2%)
    pallas_call x1, Pallas kernels, local(): pl.pallas_call(kernel, out_shape=(out, out), in_specs=[vmem, vmem, pl.Blo...  148 us
    unnamed x4, local copies, waits for them, and re-layouts  3.36 us

profile of v3, /device:TPU:1, one launch (start us, length us, event | category | flops | bytes accessed | tf_op | source)
XLA Modules:
  0.0 151.9 jit_solution(9422613121034851166)
XLA Ops:
  0.6 147.9 %shard_map.41 = (f32[16,128,128]{2,1,0:T(8,128)}, f32[16,128,128]{2,1,0:T(8,128)}) custom-call(f32[16,128,128]{2,1,0:T(8,128)} %bitcast.18, s32[4,16]{1,0:T(4,128)} %bitcast.19, s32[4,16]{1,0:T(4,128)} %bitcast.20), custom_call_target="tpu_custom_call" | custom-call | flops 1073741824 | bytes 4194304 | tf_op jit(solution)/shard_map/pallas_call | solution.py:431
  148.5 0.0 copy-start
  148.5 2.4 %copy.9 = f32[16,4,4096]{2,1,0:T(4,128)} copy(f32[16,4,4096]{2,1,0:T(4,128)} %bitcast.17) | data formatting | bytes 2097152
  150.9 0.0 copy-done
  150.9 1.0 copy.10
Async XLA Ops:
  148.5 2.4 %copy-start = (f32[16,128,128]{2,1,0:T(8,128)S(1)}, f32[16,128,128]{2,1,0:T(8,128)}, u32[]{:S(2)}) copy-start(f32[16,128,128]{2,1,0:T(8,128)} %get-tuple-element.5) | copy-start | bytes 3145732

commit v4 on v3

--- a/solution.py
+++ b/solution.py
@@ -16,15 +16,15 @@
 PIECES = 8
 STEP = ROWS // PIECES
 PIECE_US = 23.0 / PIECES
-HOP_US = 1.5
-FIND_GAP = 2.5
+HOP_US = 3.5
+FIND_US, FIND_GAP = 22.0, 2.0
 SQUARE_US = 1.1
 R_GAP, L_GAP = 3.0, 6.0
 CHUNK = 2 * ROWS
 SPAN = 2 * CHUNK + 1
 ZERO = 2 * CHUNK
 TOGETHER = 4
-GROUP = 4
+GROUP = 8
 COLS = PIECES
 
 OWN = (0, 0)
@@ -102,7 +102,7 @@
         starts.append(now)
     steps = plan(first + [("S", S_TREES, R_LINKS, starts)])
     known = max(t for t, name, _, n in steps if name != "S" and n == COLS)
-    events = [(known + 0.1 + FIND_GAP * n, "find", "", None, n) for n in range(ROWS)]
+    events = [(max(known, FIND_US) + FIND_GAP * n, "find", "", None, n) for n in range(ROWS)]
     done = {}
     for t, name, message, piece in steps:
         if name == "S" and piece == COLS or message == OWN and name != "S" and piece in (COLS, 0):
@@ -115,7 +115,7 @@
             events.append((t - SQUARE_US, "square", name, message, piece))
         else:
             events.append((t, "send", name, message, piece))
-    events += [(t + 1.5, "use", "S", message, 0) for message, t in done.items()]
+    events += [(t + 3.0, "use", "S", message, 0) for message, t in done.items()]
     events.append((starts[-1] + 0.1, "use", "S", OWN, 0))
     events.sort(key=lambda e: e[0])
     return [e[1:] for e in events]
@@ -171,9 +171,9 @@
 
 
 def kernel(
-    x_ref, cols_ref, cs_ref, sq_ref, up_ref,
-    rp, lp, acc, pc, lc, pc_s, lc_s, at_s, low_s, high_s,
-    send, cols_send, r_recv, l_recv, s_recv, r_sib, s_sib, pair_sem, local_sem,
+    x_ref, cols_ref, cs_ref, sq_out, up_out,
+    sq_ref, up_ref, rp, lp, acc, pc, lc, pc_s, lc_s, at_s, low_s, high_s,
+    send, cols_send, r_recv, l_recv, s_recv, r_sib, s_sib, pair_sem, local_sem, out_sem,
     *sp,
 ):
     place = Place()
@@ -377,7 +377,12 @@
                     store_slots(up_ref, i, lambda h, rows: acc[i, h, rows, :])
             return carry
 
-        lax.fori_loop(0, ROWS // GROUP, update_rows, 0)
+        if last:
+            for n in range(ROWS // GROUP):
+                update_rows(n, 0)
+                write_out(n + 1).start()
+        else:
+            lax.fori_loop(0, ROWS // GROUP, update_rows, 0)
 
     def follow(event):
         kind, name, message, piece = event
@@ -401,6 +406,14 @@
             lax.fori_loop(0, TOGETHER, square_piece, 0)
         elif piece >= TOGETHER:
             square_piece(piece, 0)
+            if piece == PIECES - 1:
+                write_out(0).start()
+
+    def write_out(n):
+        if n == 0:
+            return pltpu.make_async_copy(sq_ref, sq_out, out_sem.at[0])
+        rows = pl.ds((n - 1) * GROUP, GROUP)
+        return pltpu.make_async_copy(up_ref.at[rows], up_out.at[rows], out_sem.at[n])
 
     used = []
     events = whole_plan()
@@ -412,6 +425,8 @@
                 follow(event)
         follow(events.pop(0))
 
+    for n in range(ROWS // GROUP + 1):
+        write_out(n).wait()
     for name in ("R", "L", "S"):
         remote(rp.at[pl.ds(0, 7 * CHUNK)], send.at[number[name]], receive[name].at[0, 0], sibling).wait_send()
     for name in ("R", "S"):
@@ -432,8 +447,10 @@
         kernel,
         out_shape=(out, out),
         in_specs=[vmem, vmem, pl.BlockSpec(memory_space=pltpu.SMEM)],
-        out_specs=(vmem, vmem),
+        out_specs=(pl.BlockSpec(memory_space=pl.ANY),) * 2,
         scratch_shapes=[
+            pltpu.VMEM((ROWS, 128, 128), jnp.float32),
+            pltpu.VMEM((ROWS, 128, 128), jnp.float32),
             pltpu.VMEM((N_R // 2 * SPAN, 64, 128), jnp.float32),
             pltpu.VMEM((N_C, ROWS, 2, 64, 128), jnp.float32),
             pltpu.VMEM((ROWS, 2, 64, 128), jnp.float32),
@@ -453,6 +470,7 @@
             dma((8,)),
             dma((1,)),
             dma((2,)),
+            dma((ROWS // GROUP + 1,)),
         ]
         + [pltpu.VMEM((SPAN, 64, 128), jnp.float32)] * 8,
         compiler_params=pltpu.CompilerParams(

time: 152 us -> 144 us (0.947)
  Pallas kernels: 148 us -> 140 us
    pallas_call x1, Pallas kernels: 148 us -> 140 us  [local(): pl.pallas_call(kernel, out_shape=(out, out), in_specs=[vmem, vmem, pl.Blo...]
where the time goes in v4:
time: 144 us
  Pallas kernels  140 us (97%)
  local copies, waits for them, and re-layouts  3.36 us (2%)
    pallas_call x1, Pallas kernels, local(): pl.pallas_call(kernel, out_shape=(out, out), in_specs=[vmem, vmem, pl.Blo...  140 us
    unnamed x4, local copies, waits for them, and re-layouts  3.36 us

profile of v4, /device:TPU:1, one launch (start us, length us, event | category | flops | bytes accessed | tf_op | source)
XLA Modules:
  0.0 144.2 jit_solution(8763177181025714870)
XLA Ops:
  0.6 140.2 %shard_map.41 = (f32[16,128,128]{2,1,0:T(8,128)}, f32[16,128,128]{2,1,0:T(8,128)}) custom-call(f32[16,128,128]{2,1,0:T(8,128)} %bitcast.18, s32[4,16]{1,0:T(4,128)} %bitcast.19, s32[4,16]{1,0:T(4,128)} %bitcast.20), custom_call_target="tpu_custom_call" | custom-call | flops 1073741824 | bytes 4194304 | tf_op jit(solution)/shard_map/pallas_call | solution.py:446
  140.8 0.0 copy-start
  140.8 2.4 %copy.9 = f32[16,4,4096]{2,1,0:T(4,128)} copy(f32[16,4,4096]{2,1,0:T(4,128)} %bitcast.17) | data formatting | bytes 2097152
  143.2 0.0 copy-done
  143.2 1.0 copy.10
Async XLA Ops:
  140.8 2.4 %copy-start = (f32[16,128,128]{2,1,0:T(8,128)S(1)}, f32[16,128,128]{2,1,0:T(8,128)}, u32[]{:S(2)}) copy-start(f32[16,128,128]{2,1,0:T(8,128)} %get-tuple-element.5) | copy-start | bytes 3145732
